TPU v7x, 32 devices: a whole 2x2x4 slice. The times are simulated.
32 devices in a mesh: grp: 2 (over x), ty: 16 (over z, y, core).
Axes of the slice: x: 2, y: 2, z: 4, core: 2. Of those that a mesh axis runs over, the one named last changes fastest.
Arguments:
- tile_object: float32 [4, 2, 4096, 768], P(None, None, ('grp', 'ty')), parts along dimension 2, may hold values from -6 to 6
- probe_wave: float32 [2, 128, 128], replicated, may hold values from -6 to 6
- propagator_phase: float32 [128, 128], replicated, may hold values from -3.140625 to 3.140625
- diffraction: float32 [128, 128, 128], P(('grp', 'ty')), parts along dimension 0, may hold values from 0 to 2
- positions: int32 [128, 2], P(('grp', 'ty')), parts along dimension 0, may hold values from 0 to 640, as said below
- counts: int32 [32], P(('grp', 'ty')), parts along dimension 0, may hold values from 0 to 4, as said below
Outputs:
- object_grad: float32 [4, 2, 4096, 768], P(None, None, ('grp', 'ty')), parts along dimension 2
There are 2 independent parts, one for each index of `grp`. A program takes and returns all parts, laid end to end along the dimension named above; an argument that names none is the same for every part. Nothing has to cross between parts.
Inputs may be any that keep to these rules, and one draw needn't show every extreme that they name: `positions`: column 0 is a row offset under 128, column 1 a column offset of at most 640. For every device d, the counts of devices 0 to d sum to between 2 * (d + 1) and 2 * (d + 2), the upper bound reached at some device; all counts sum to 32.
All inputs are finite; a program needn't handle non-finite values.
Results may differ from a plain program's by a relative error of at most 0.0003.
Values sent between devices are 32-bit elements; how exact they have to be, the bound alone decides.
No kernel may reach another device: no remote copies, remote signals or barrier semaphores. Data moves between devices by JAX's collectives and lax.ppermute only.
A program may use at most 64 MiB of HBM per device.

v0:
```python
import functools

import jax
import jax.numpy as jnp
import ml_dtypes
import numpy as np
from jax import lax
from jax.experimental import pallas as pl
from jax.experimental.pallas import tpu as pltpu
from jax.sharding import PartitionSpec as P

PS = 128
PLANES = 8
SLOTS = 4
CAP = 160
F32 = jnp.float32

N_KEPT, N_MOVED = 0, 1
KEPT, MOVED = 2, 18
PLAN = 128

CHAINS = 4
PACK_VMEM = 8 * 1024 * 1024
WAVE_VMEM = 20 * 1024 * 1024


def shifted(x, axis, by):
    peers = lax.axis_size(axis)
    return lax.ppermute(x, axis, [(i, (i + by) % peers) for i in range(peers)])


def dft_tables():
    index = np.arange(PS)
    angle = 2.0 * np.pi * (index[:, None] * index[None, :] % PS) / PS
    re, im = np.cos(angle) / np.sqrt(PS), -np.sin(angle) / np.sqrt(PS)
    fwd = np.block([[re, im], [-im, re]])
    tables = []
    for full in (fwd, fwd.T):
        high = full.astype(ml_dtypes.bfloat16)
        tables += [high, (full - high.astype(np.float64)).astype(ml_dtypes.bfloat16)]
    return np.stack(tables)


def write_plan(pos_ref, count_ref, plan_ref):
    count = count_ref[0]
    rows = [pos_ref[0, j] for j in range(SLOTS)]
    best_score, best_set = jnp.int32(1 << 30), jnp.int32(0)
    for chosen in range(1 << SLOTS):
        up = down = kept = moved = jnp.int32(0)
        for j in range(SLOTS):
            live = (count > j).astype(jnp.int32)
            if chosen >> j & 1:
                down, moved = down + live * (PS - rows[j]), moved + live
            else:
                up, kept = up + live * rows[j], kept + live
        most = jnp.maximum(up, down)
        score = (
            most
            + jnp.where(most > CAP, 1 << 20, 0)
            + jnp.where(kept > 2, 1 << 10, 0)
            + jnp.where(moved > 2, 1 << 10, 0)
        )
        better = score < best_score
        best_score = jnp.where(better, score, best_score)
        best_set = jnp.where(better, chosen, best_set)
    for j in range(SLOTS):
        for base in (KEPT, MOVED):
            for field in range(4):
                plan_ref[base + 4 * field + j] = 0
    n = [jnp.int32(0), jnp.int32(0)]
    offset = [jnp.int32(0), jnp.int32(0)]
    spare = PLAN - 16
    for j in range(SLOTS):
        live = count > j
        moved = (best_set >> j) & 1
        for side, base in ((0, KEPT), (1, MOVED)):
            mine = jnp.logical_and(live, moved == side)
            at = jnp.where(mine, base + n[side], spare)
            plan_ref[at] = rows[j]
            plan_ref[at + 4] = pos_ref[1, j]
            plan_ref[at + 8] = offset[side]
            plan_ref[at + 12] = j
            taken = PS - rows[j] if side else rows[j]
            n[side] = n[side] + mine.astype(jnp.int32)
            offset[side] = offset[side] + jnp.where(mine, taken, 0)
    plan_ref[N_KEPT] = n[0]
    plan_ref[N_MOVED] = n[1]


def lanes():
    return lax.broadcasted_iota(jnp.int32, (PS, PS), 1)


def sublanes():
    return lax.broadcasted_iota(jnp.int32, (PS, PS), 0)


def column_blocks(col, width):
    first = pl.multiple_of((col // PS) * PS, PS)
    second = pl.multiple_of(jnp.minimum(first + PS, width - PS), PS)
    return first, second, col % PS


def shifted_columns(left, right, by):
    back = (PS - by) & (PS - 1)
    return jnp.where(lanes() < PS - by, pltpu.roll(left, back, 1), pltpu.roll(right, back, 1))


def read_columns(ref, plane, col):
    first, second, part = column_blocks(col, ref.shape[-1])
    return shifted_columns(ref[plane, :, pl.ds(first, PS)], ref[plane, :, pl.ds(second, PS)], part)


def add_columns(ref, plane, col, value):
    first, second, part = column_blocks(col, ref.shape[-1])
    value = pltpu.roll(value, part, 1)
    here = lanes() >= part
    ref[plane, :, pl.ds(first, PS)] += jnp.where(here, value, 0.0)
    ref[plane, :, pl.ds(second, PS)] += jnp.where(here, 0.0, value)


def entry(plan_ref, base, k):
    return plan_ref[base + k], plan_ref[base + 4 + k], plan_ref[base + 8 + k]


def pack_moved_kernel(pos_ref, count_ref, tile_ref, packed_ref, plan, columns, packed, sems):
    write_plan(pos_ref, count_ref, plan)
    count = plan[N_MOVED]

    def fetch(k):
        start = pl.multiple_of(plan[MOVED + 4 + k] // PS * PS, PS)
        start = pl.multiple_of(jnp.minimum(start, tile_ref.shape[2] - 2 * PS), PS)
        source = tile_ref.at[:, :, pl.ds(start, 2 * PS)]
        return pltpu.make_async_copy(source, columns.at[k], sems.at[k]), start

    for k in range(SLOTS):

        @pl.when(k < count)
        def _(k=k):
            fetch(k)[0].start()

    for k in reversed(range(SLOTS)):

        @pl.when(k < count)
        def _(k=k):
            row, col, offset = entry(plan, MOVED, k)
            copy, start = fetch(k)
            copy.wait()
            for plane in range(PLANES):
                value = shifted_columns(
                    columns[k, plane, :, :PS], columns[k, plane, :, PS:], col - start
                )
                packed[plane, pl.ds(PS + offset - row, PS), :] = value

    packed_ref[...] = packed[:, PS : PS + CAP, :]


def pack_moved(positions, counts, tile):
    planes, rows, _ = tile.shape
    smem = pl.BlockSpec(memory_space=pltpu.SMEM)
    return pl.pallas_call(
        pack_moved_kernel,
        out_shape=jax.ShapeDtypeStruct((planes, CAP, PS), F32),
        in_specs=[smem, smem, pl.BlockSpec(memory_space=pl.ANY)],
        out_specs=pl.BlockSpec(memory_space=pltpu.VMEM),
        scratch_shapes=[
            pltpu.SMEM((PLAN,), jnp.int32),
            pltpu.VMEM((SLOTS, planes, rows, 2 * PS), F32),
            pltpu.VMEM((planes, CAP + 2 * PS, PS), F32),
            pltpu.SemaphoreType.DMA((SLOTS,)),
        ],
        compiler_params=pltpu.CompilerParams(vmem_limit_bytes=PACK_VMEM),
        cost_estimate=pl.CostEstimate(flops=0, bytes_accessed=4 * 1024 * 1024, transcendentals=0),
        name="pack_moved",
    )(positions, counts, tile)


def parts_kernel(
    pos_ref, count_ref, pos_above_ref, count_above_ref, tile_ref,
    packed_ref, kept_ref, moved_ref, plan, above, packed,
):
    write_plan(pos_above_ref, count_above_ref, above)

    @pl.loop(0, above[N_KEPT])
    def _(k):
        _, col, offset = entry(above, KEPT, k)
        for plane in range(PLANES):
            packed[plane, pl.ds(offset, PS), :] = read_columns(tile_ref, plane, col)

    packed_ref[...] = packed[:, :CAP, :]
    write_plan(pos_ref, count_ref, plan)

    @pl.loop(0, plan[N_KEPT])
    def _(k):
        for plane in range(PLANES):
            kept_ref[k, plane] = read_columns(tile_ref, plane, plan[KEPT + 4 + k])

    @pl.loop(0, above[N_MOVED])
    def _(k):
        for plane in range(PLANES):
            moved_ref[k, plane] = read_columns(tile_ref, plane, above[MOVED + 4 + k])


def parts(where, tile):
    planes = tile.shape[0]
    smem = pl.BlockSpec(memory_space=pltpu.SMEM)
    vmem = pl.BlockSpec(memory_space=pltpu.VMEM)
    windows = jax.ShapeDtypeStruct((SLOTS, planes, PS, PS), F32)
    return pl.pallas_call(
        parts_kernel,
        out_shape=(jax.ShapeDtypeStruct((planes, CAP, PS), F32), windows, windows),
        in_specs=[smem] * 4 + [vmem],
        out_specs=(vmem, vmem, vmem),
        scratch_shapes=[
            pltpu.SMEM((PLAN,), jnp.int32),
            pltpu.SMEM((PLAN,), jnp.int32),
            pltpu.VMEM((planes, CAP + PS, PS), F32),
        ],
        compiler_params=pltpu.CompilerParams(vmem_limit_bytes=PACK_VMEM),
        cost_estimate=pl.CostEstimate(flops=0, bytes_accessed=8 * 1024 * 1024, transcendentals=0),
        name="parts",
    )(*where, tile)


def split(x):
    high = x.astype(jnp.bfloat16)
    return high, (x - high.astype(F32)).astype(jnp.bfloat16)


def dot(a, b):
    return jnp.dot(a, b, preferred_element_type=F32)


def times_table(x, table):
    high, low = split(x)
    return dot(low, table[0]) + dot(high, table[1]) + dot(high, table[0])


def turned(x):
    return jnp.concatenate([x[:, :PS].T, x[:, PS:].T], axis=1)


def halves(x):
    return x[:, :PS], x[:, PS:]


def times(a, b):
    (a_re, a_im), (b_re, b_im) = a, b
    return jnp.concatenate([a_re * b_re - a_im * b_im, a_re * b_im + a_im * b_re], axis=1)


def times_conj(a, b):
    (a_re, a_im), (b_re, b_im) = a, b
    return jnp.concatenate([a_re * b_re + a_im * b_im, a_im * b_re - a_re * b_im], axis=1)


def wave_kernel(
    moved, pos_ref, count_ref, own_ref, msg_ref, pattern_ref, probe_ref, prop_ref, table_ref,
    *refs,
):
    grads_ref, out_ref, plan_ref, msg, patch, grad, waves, packed = refs[-8:]
    write_plan(pos_ref, count_ref, plan_ref)
    msg[:, :CAP, :] = msg_ref[...]
    base = MOVED if moved else KEPT
    count = plan_ref[N_MOVED if moved else N_KEPT]
    layers = PLANES // 2
    chains = range(patch.shape[0])
    fwd = (table_ref[0], table_ref[1])
    bwd = (table_ref[2], table_ref[3])

    def transform(xs, table):
        return [times_table(turned(times_table(x, table)), table) for x in xs]

    def propagate(xs, product):
        prop = (prop_ref[0], prop_ref[1])
        xs = [product(halves(x), prop) for x in transform(xs, fwd)]
        return transform(xs, bwd)

    def layer_of(i, layer):
        return patch[i, 2 * layer, PS : 2 * PS, :], patch[i, 2 * layer + 1, PS : 2 * PS, :]

    @pl.loop(0, (count + len(chains) - 1) // len(chains))
    def _(group):
        first = group * len(chains)
        for i in chains:

            @pl.when(first + i < count)
            def _(i=i, k=first + i):
                row, _, offset = entry(plan_ref, base, k)
                for plane in range(PLANES):
                    own, other = own_ref[k, plane], msg[plane, pl.ds(offset, PS), :]
                    if moved:
                        patch[i, plane, PS : 2 * PS, :] = other
                        patch[i, plane, pl.ds(2 * PS - row, PS), :] = own
                    else:
                        patch[i, plane, pl.ds(PS - row, PS), :] = own
                        patch[i, plane, pl.ds(2 * PS - row, PS), :] = other

        probe = (probe_ref[0], probe_ref[1])
        for layer in range(layers):
            xs = []
            for i in chains:
                wave = halves(waves[layer, i]) if layer else probe
                xs.append(times(wave, layer_of(i, layer)))
            if layer + 1 < layers:
                for i, x in enumerate(propagate(xs, times)):
                    waves[layer + 1, i] = x
        xs = transform(xs, fwd)
        for i in chains:
            slot = plan_ref[base + 12 + jnp.minimum(first + i, SLOTS - 1)]
            re, im = halves(xs[i])
            scale = 4.0 * (re * re + im * im - pattern_ref[slot].T)
            xs[i] = jnp.concatenate([scale * re, scale * im], axis=1)
        xs = transform(xs, bwd)
        for layer in reversed(range(layers)):
            for i in chains:
                wave = halves(waves[layer, i]) if layer else probe
                d_re, d_im = halves(times_conj(halves(xs[i]), wave))
                grad[i, 2 * layer, :PS, :] = d_re
                grad[i, 2 * layer + 1, :PS, :] = d_im
                if layer:
                    xs[i] = times_conj(halves(xs[i]), layer_of(i, layer))
            if layer:
                xs = propagate(xs, times_conj)

        for i in chains:

            @pl.when(first + i < count)
            def _(i=i, k=first + i):
                row, _, offset = entry(plan_ref, base, k)
                grads_ref[k] = grad[i, :, :PS, :]
                for plane in range(PLANES):
                    start = 0 if moved else PS - row
                    packed[plane, pl.ds(offset, PS), :] = grad[i, plane, pl.ds(start, PS), :]

    out_ref[...] = packed[:, :CAP, :]


def gradients(moved, positions, counts, own, msg, patterns, probe, prop, tables, after=()):
    planes = own.shape[1]
    smem = pl.BlockSpec(memory_space=pltpu.SMEM)
    vmem = pl.BlockSpec(memory_space=pltpu.VMEM)
    return pl.pallas_call(
        functools.partial(wave_kernel, moved),
        out_shape=(
            jax.ShapeDtypeStruct((SLOTS, planes, PS, PS), F32),
            jax.ShapeDtypeStruct((planes, CAP, PS), F32),
        ),
        in_specs=[smem] * 2 + [vmem] * 6 + [pl.BlockSpec(memory_space=pl.ANY)] * len(after),
        out_specs=(vmem, vmem),
        scratch_shapes=[
            pltpu.SMEM((PLAN,), jnp.int32),
            pltpu.VMEM((planes, CAP + PS, PS), F32),
            pltpu.VMEM((CHAINS, planes, 3 * PS, PS), F32),
            pltpu.VMEM((CHAINS, planes, 2 * PS, PS), F32),
            pltpu.VMEM((planes // 2, CHAINS, PS, 2 * PS), F32),
            pltpu.VMEM((planes, CAP + PS, PS), F32),
        ],
        compiler_params=pltpu.CompilerParams(vmem_limit_bytes=WAVE_VMEM),
        cost_estimate=pl.CostEstimate(
            flops=6 * 1024**3, bytes_accessed=8 * 1024 * 1024, transcendentals=0
        ),
        name="waves_moved" if moved else "waves_kept",
    )(positions, counts, own, msg, patterns, probe, prop, tables, *after)


def deposit_kernel(
    pos_ref, count_ref, pos_above_ref, count_above_ref, kept_ref, moved_ref, below_ref, out_ref, plan, above, shift
):
    write_plan(pos_ref, count_ref, plan)
    write_plan(pos_above_ref, count_above_ref, above)
    out_ref[...] = jnp.zeros_like(out_ref)

    @pl.loop(0, plan[N_KEPT])
    def _(k):
        row, col, _ = entry(plan, KEPT, k)
        inside = sublanes() >= row
        for plane in range(PLANES):
            shift[plane, pl.ds(row, PS), :] = kept_ref[k, plane]
            add_columns(out_ref, plane, col, jnp.where(inside, shift[plane, :PS, :], 0.0))

    @pl.loop(0, above[N_MOVED])
    def _(k):
        row, col, _ = entry(above, MOVED, k)
        inside = sublanes() < row
        for plane in range(PLANES):
            shift[plane, pl.ds(row, PS), :] = moved_ref[k, plane]
            add_columns(out_ref, plane, col, jnp.where(inside, shift[plane, PS : 2 * PS, :], 0.0))

    shift[:, PS : PS + CAP, :] = below_ref[...]

    @pl.loop(0, plan[N_MOVED])
    def _(k):
        row, col, offset = entry(plan, MOVED, k)
        inside = sublanes() >= row
        for plane in range(PLANES):
            value = shift[plane, pl.ds(PS + offset - row, PS), :]
            add_columns(out_ref, plane, col, jnp.where(inside, value, 0.0))


def deposit(where, kept, moved, from_below, shape):
    planes = shape[0]
    smem = pl.BlockSpec(memory_space=pltpu.SMEM)
    vmem = pl.BlockSpec(memory_space=pltpu.VMEM)
    return pl.pallas_call(
        deposit_kernel,
        out_shape=jax.ShapeDtypeStruct(shape, F32),
        in_specs=[smem] * 4 + [vmem] * 3,
        out_specs=vmem,
        scratch_shapes=[pltpu.SMEM((PLAN,), jnp.int32)] * 2
        + [pltpu.VMEM((planes, CAP + 2 * PS, PS), F32)],
        compiler_params=pltpu.CompilerParams(vmem_limit_bytes=PACK_VMEM),
        cost_estimate=pl.CostEstimate(flops=0, bytes_accessed=4 * 1024 * 1024, transcendentals=0),
        name="deposit",
    )(*where, kept, moved, from_below)


def finish_kernel(pos_ref, count_ref, sum_ref, msg_ref, out_ref, plan, total, msg, sems):
    write_plan(pos_ref, count_ref, plan)
    msg[:, :CAP, :] = msg_ref[...]
    copies = []
    for plane in range(PLANES):
        total[plane] = sum_ref[plane]

        @pl.loop(0, plan[N_KEPT])
        def _(k, plane=plane):
            row, col, offset = entry(plan, KEPT, k)
            value = jnp.where(sublanes() < row, msg[plane, pl.ds(offset, PS), :], 0.0)
            add_columns(total, plane, col, value)

        copy = pltpu.make_async_copy(total.at[plane], out_ref.at[plane], sems.at[plane])
        copy.start()
        copies.append(copy)
    for copy in copies:
        copy.wait()


def finish(positions_above, counts_above, summed, from_above):
    planes = summed.shape[0]
    smem = pl.BlockSpec(memory_space=pltpu.SMEM)
    vmem = pl.BlockSpec(memory_space=pltpu.VMEM)
    return pl.pallas_call(
        finish_kernel,
        out_shape=jax.ShapeDtypeStruct(summed.shape, F32),
        in_specs=[smem, smem, vmem, vmem],
        out_specs=pl.BlockSpec(memory_space=pl.ANY),
        scratch_shapes=[
            pltpu.SMEM((PLAN,), jnp.int32),
            pltpu.VMEM(summed.shape, F32),
            pltpu.VMEM((planes, CAP + PS, PS), F32),
            pltpu.SemaphoreType.DMA((planes,)),
        ],
        compiler_params=pltpu.CompilerParams(vmem_limit_bytes=PACK_VMEM),
        cost_estimate=pl.CostEstimate(flops=0, bytes_accessed=4 * 1024 * 1024, transcendentals=0),
        name="finish",
    )(positions_above, counts_above, summed, from_above)


def per_device(tile_object, probe_wave, propagator_phase, diffraction, positions, counts):
    layers, two, rows, width = tile_object.shape
    tile = tile_object.reshape(layers * two, rows, width)
    positions = positions.T
    positions_above = shifted(positions, "ty", 1)
    counts_above = shifted(counts, "ty", 1)
    patterns_above = shifted(diffraction, "ty", 1)
    phase = propagator_phase.T
    prop = jnp.stack([jnp.cos(phase), jnp.sin(phase)])
    tables = jnp.asarray(dft_tables())

    down = pack_moved(positions, counts, tile)
    down, positions_above, counts_above, patterns_above = lax.optimization_barrier(
        (down, positions_above, counts_above, patterns_above)
    )
    rows_above = shifted(down, "ty", 1)
    where = (positions, counts, positions_above, counts_above)
    up, own_kept, own_moved = parts(where, tile)
    up, rows_above = lax.optimization_barrier((up, rows_above))
    rows_below = shifted(up, "ty", -1)
    moved, back_up = gradients(
        True, positions_above, counts_above, own_moved, rows_above, patterns_above,
        probe_wave, prop, tables,
    )
    from_below = shifted(back_up, "ty", -1)
    kept, back_down = gradients(
        False, positions, counts, own_kept, rows_below, diffraction,
        probe_wave, prop, tables, after=(moved,),
    )
    from_above = shifted(back_down, "ty", 1)
    summed = deposit(where, kept, moved, from_below, tile.shape)
    out = finish(positions_above, counts_above, summed, from_above)
    return out.reshape(tile_object.shape)


def solution(mesh):
    in_specs = (
        P(None, None, ("grp", "ty"), None),
        P(),
        P(),
        P(("grp", "ty"), None, None),
        P(("grp", "ty"), None),
        P(("grp", "ty")),
    )
    out_specs = P(None, None, ("grp", "ty"), None)
    return jax.shard_map(
        per_device, mesh=mesh, in_specs=in_specs, out_specs=out_specs, check_vma=False
    )
```

profile of v0, /device:TPU:0, one launch (start us, length us, event | category | flops | bytes accessed | tf_op | source)
XLA Modules:
  0.0 55.6 jit_solution(15306850827034025471)
XLA Ops:
  0.0 0.0 copy-start.3
  0.0 0.5 collective-permute-start.2
  0.5 2.6 %collective-permute-start.1 = (s32[1]{0:T(128)}, s32[1]{0:T(128)}, u32[]{:S(2)}, u32[]{:S(2)}) collective-permute-start(s32[1]{0:T(128)} %param.12), channel_id=1, source_target_pairs={{0,1},{1,2},{2,3},{3,4},{4,5},{5,6},{6,7},{7,8},{8,9},{9,10},{10,1... | collective-permute-start | bytes 20 | tf_op jit(solution)/shard_map/ppermute | solution.py:29
  3.1 0.0 collective-permute-start
  3.8 0.0 copy-start
  3.8 1.9 %copy-done = f32[4,2,128,768]{3,2,1,0:T(8,128)S(1)} copy-done((f32[4,2,128,768]{3,2,1,0:T(8,128)S(1)}, f32[4,2,128,768]{3,2,1,0:T(8,128)}, u32[]{:S(2)}) %copy-start) | copy-done | bytes 3145752
  5.7 0.0 copy-start.2
  5.7 0.7 %copy-done.2 = s32[4,2]{0,1:T(2,128)S(1)} copy-done((s32[4,2]{0,1:T(2,128)S(1)}, s32[4,2]{0,1:T(2,128)}, u32[]{:S(2)}) %copy-start.2) | copy-done | bytes 56
  6.4 0.0 copy-start.1
  6.4 2.4 %pack_moved.1 = f32[8,160,128]{2,1,0:T(8,128)} custom-call(s32[2,4]{1,0:T(2,128)S(1)} %bitcast.14, s32[1]{0:T(128)S(6)} %copy.10.count_ref, f32[8,128,768]{2,1,0:T(8,128)S(1)} %bitcast.11), custom_call_target="tpu_custom_call" | custom-call | bytes 4194304 | tf_op jit(solution)/shard_map/pack_moved/pallas_call | solution.py:161
  8.8 0.0 copy-start.5
  8.8 1.1 %collective-permute-done.1.count_above_ref.count_ref = s32[1]{0:T(128)} collective-permute-done((s32[1]{0:T(128)}, s32[1]{0:T(128)}, u32[]{:S(2)}, u32[]{:S(2)}) %collective-permute-start.1) | collective-permute-done | bytes 36 | tf_op jit(solution)/shard_map/ppermute | solution.py:29
  9.9 0.0 collective-permute-done.pos_above_ref.pos_ref
  9.9 0.0 collective-permute-done.2.pattern_ref
  9.9 0.0 collective-permute-start.3
  9.9 1.6 %copy.8 = f32[128,128]{0,1:T(8,128)} copy(f32[128,128]{1,0:T(8,128)} %param.9) | data formatting | bytes 131072 | tf_op args[2]
  11.5 0.0 copy-start.6
  11.5 1.1 %cosine_bitcast_fusion = (f32[1,128,128]{2,1,0:T(8,128)S(1)}, f32[1,128,128]{2,1,0:T(8,128)S(1)}) fusion(f32[128,128]{0,1:T(8,128)} %copy.8), kind=kLoop, calls=%fused_computation.2 | loop fusion | bytes 196608 | tf_op jit(solution)/shard_map/stack | solution.py:467
  12.6 0.0 copy-done.3
  12.6 0.0 copy-done.1
  12.6 2.1 %parts.1 = (f32[8,160,128]{2,1,0:T(8,128)S(1)}, f32[4,8,128,128]{3,2,1,0:T(8,128)S(1)}, f32[4,8,128,128]{3,2,1,0:T(8,128)S(1)}) custom-call(s32[2,4]{1,0:T(2,128)S(1)} %bitcast.15, s32[1]{0:T(128)S(6)} %copy.10.count_ref, s32[2,4]{1,0:T(2,128)S(1)} %collective-permute-done.pos_above_ref.pos_ref, s32[1]{0:T(128)} %collective-permute-done.1.count_above_ref.count_ref, ...), custom_call_target="tpu_custom_call" | custom-call | bytes 8388608 | tf_op jit(solution)/shard_map/parts/pallas_call | solution.py:209
  14.7 8.3 %collective-permute-done.3.msg_ref = f32[8,160,128]{2,1,0:T(8,128)} collective-permute-done((f32[8,160,128]{2,1,0:T(8,128)}, f32[8,160,128]{2,1,0:T(8,128)}, u32[]{:S(2)}, u32[]{:S(2)}) %collective-permute-start.3) | collective-permute-done | bytes 655392 | tf_op jit(solution)/shard_map/ppermute | solution.py:29
  23.0 0.0 collective-permute-start.4
  23.0 0.0 copy-done.5
  23.0 0.0 copy-done.6
  23.0 0.0 copy-start.4
  23.0 1.9 %waves_moved.1 = (f32[4,8,128,128]{3,2,1,0:T(8,128)S(1)}, f32[8,160,128]{2,1,0:T(8,128)S(1)}) custom-call(s32[2,4]{1,0:T(2,128)S(1)} %collective-permute-done.pos_above_ref.pos_ref, s32[1]{0:T(128)} %collective-permute-done.1.count_above_ref.count_ref, f32[4,8,128,128]{3,2,1,0:T(8,128)S(1)} %get-tuple-element.24.own_ref, ...), custom_call_target="tpu_custom_call" | custom-call | flops 6442450944 | bytes 8388608 | tf_op jit(solution)/shard_map/waves_moved/pallas_call | solution.py:343
  24.9 6.8 %collective-permute-start.5 = (f32[8,160,128]{2,1,0:T(8,128)S(1)}, f32[8,160,128]{2,1,0:T(8,128)S(1)}, u32[]{:S(2)}, u32[]{:S(2)}) collective-permute-start(f32[8,160,128]{2,1,0:T(8,128)S(1)} %get-tuple-element.29), channel_id=1, source_target_pairs={{0,15},{1,0},{2,1},{3,2},{4,3},{5,4},{6,5},{7,6},{8,7},{9,8},{10,9... | collective-permute-start | bytes 1966088 | tf_op jit(solution)/shard_map/ppermute | solution.py:29
  31.7 0.0 collective-permute-done.4.msg_ref
  31.7 0.0 copy-done.4
  31.7 8.0 %waves_kept.1 = (f32[4,8,128,128]{3,2,1,0:T(8,128)S(1)}, f32[8,160,128]{2,1,0:T(8,128)S(1)}) custom-call(s32[2,4]{1,0:T(2,128)S(1)} %bitcast.16, s32[1]{0:T(128)S(6)} %copy.10.count_ref, f32[4,8,128,128]{3,2,1,0:T(8,128)S(1)} %get-tuple-element.20.own_ref, f32[8,160,128]{2,1,0:T(8,128)S(1)} %collective-permute-done.4.msg_ref, f32[4,128,128]{2,1,0:T(8,128)S(1)} %copy-done.4, ...), custom_call_target="tpu_custom_call" | custom-call | flops 6442450944 | bytes 8388608 | tf_op jit(solution)/shard_map/waves_kept/pallas_call | solution.py:343
  39.7 0.1 collective-permute-start.6
  39.8 0.0 collective-permute-done.5.below_ref
  39.8 2.6 %deposit.1.sum_ref = f32[8,128,768]{2,1,0:T(8,128)S(1)} custom-call(s32[2,4]{1,0:T(2,128)S(1)} %bitcast.17, s32[1]{0:T(128)S(6)} %copy.10.count_ref, s32[2,4]{1,0:T(2,128)S(1)} %collective-permute-done.pos_above_ref.pos_ref, s32[1]{0:T(128)} %collective-permute-done.1.count_above_ref.count_ref, f32[4,8,128,128]{3,2,1,0:T(8,128)S(1)} %get-tuple-element.28.kept_ref, ...), custom_call_target="tpu_custom_call" | custom-call | bytes 4194304 | tf_op jit(solution)/shard_map/deposit/pallas_call | solution.py:405
  42.4 10.1 %collective-permute-done.6.msg_ref = f32[8,160,128]{2,1,0:T(8,128)S(1)} collective-permute-done((f32[8,160,128]{2,1,0:T(8,128)S(1)}, f32[8,160,128]{2,1,0:T(8,128)S(1)}, u32[]{:S(2)}, u32[]{:S(2)}) %collective-permute-start.6) | collective-permute-done | bytes 655392 | tf_op jit(solution)/shard_map/ppermute | solution.py:29
  52.5 2.9 %finish.1 = f32[8,128,768]{2,1,0:T(8,128)} custom-call(s32[2,4]{1,0:T(2,128)S(1)} %collective-permute-done.pos_above_ref.pos_ref, s32[1]{0:T(128)} %collective-permute-done.1.count_above_ref.count_ref, f32[8,128,768]{2,1,0:T(8,128)S(1)} %deposit.1.sum_ref, f32[8,160,128]{2,1,0:T(8,128)S(1)} %collective-permute-done.6.msg_ref), custom_call_target="tpu_custom_call" | custom-call | bytes 4194304 | tf_op jit(solution)/shard_map/finish/pallas_call | solution.py:442
  (1 shorter events, 0.0 us)
Async XLA Ops:
  0.0 12.6 %copy-start.3 = (s32[4,2]{0,1:T(2,128)S(1)}, s32[4,2]{0,1:T(2,128)}, u32[]{:S(2)}) copy-start(s32[4,2]{0,1:T(2,128)} %param.11) | copy-start | bytes 100
  0.0 9.9 %collective-permute-start.2 = (f32[4,128,128]{2,1,0:T(8,128)}, f32[4,128,128]{2,1,0:T(8,128)S(1)}, u32[]{:S(2)}, u32[]{:S(2)}) collective-permute-start(f32[4,128,128]{2,1,0:T(8,128)} %pattern_ref.1), channel_id=1, source_target_pairs={{0,1},{1,2},{2,3},{3,4},{4,5},{5,6},{6,7},{7,8},{8,9},{9,10},{10,1... | collective-permute-start | bytes 786440 | tf_op jit(solution)/shard_map/ppermute | solution.py:29
  0.5 9.4 %collective-permute-start.1 = (s32[1]{0:T(128)}, s32[1]{0:T(128)}, u32[]{:S(2)}, u32[]{:S(2)}) collective-permute-start(s32[1]{0:T(128)} %param.12), channel_id=1, source_target_pairs={{0,1},{1,2},{2,3},{3,4},{4,5},{5,6},{6,7},{7,8},{8,9},{9,10},{10,1... | collective-permute-start | bytes 20 | tf_op jit(solution)/shard_map/ppermute | solution.py:29
  3.1 6.8 %collective-permute-start = (s32[2,4]{1,0:T(2,128)}, s32[2,4]{1,0:T(2,128)S(1)}, u32[]{:S(2)}, u32[]{:S(2)}) collective-permute-start(s32[2,4]{1,0:T(2,128)} %bitcast.13), channel_id=1, source_target_pairs={{0,1},{1,2},{2,3},{3,4},{4,5},{5,6},{6,7},{7,8},{8,9},{9,10},{10,1... | collective-permute-start | bytes 104 | tf_op jit(solution)/shard_map/ppermute | solution.py:29
  3.8 1.9 %copy-start = (f32[4,2,128,768]{3,2,1,0:T(8,128)S(1)}, f32[4,2,128,768]{3,2,1,0:T(8,128)}, u32[]{:S(2)}) copy-start(f32[4,2,128,768]{3,2,1,0:T(8,128)} %param.7) | copy-start | bytes 9437188
  5.7 0.7 %copy-start.2 = (s32[4,2]{0,1:T(2,128)S(1)}, s32[4,2]{0,1:T(2,128)}, u32[]{:S(2)}) copy-start(s32[4,2]{0,1:T(2,128)} %param.11) | copy-start | bytes 100
  6.4 6.3 %copy-start.1 = (f32[4,2,128,768]{3,2,1,0:T(8,128)S(1)}, f32[4,2,128,768]{3,2,1,0:T(8,128)}, u32[]{:S(2)}) copy-start(f32[4,2,128,768]{3,2,1,0:T(8,128)} %param.7) | copy-start | bytes 9437188
  8.8 14.2 %copy-start.5 = (f32[2,128,128]{2,1,0:T(8,128)S(1)}, f32[2,128,128]{2,1,0:T(8,128)}, u32[]{:S(2)}) copy-start(f32[2,128,128]{2,1,0:T(8,128)} %probe_ref.3) | copy-start | bytes 393220
  9.9 13.1 %collective-permute-start.3 = (f32[8,160,128]{2,1,0:T(8,128)}, f32[8,160,128]{2,1,0:T(8,128)}, u32[]{:S(2)}, u32[]{:S(2)}) collective-permute-start(f32[8,160,128]{2,1,0:T(8,128)} %pack_moved.1), channel_id=1, source_target_pairs={{0,1},{1,2},{2,3},{3,4},{4,5},{5,6},{6,7},{7,8},{8,9},{9,10},{10,1... | collective-permute-start | bytes 1966088 | tf_op jit(solution)/shard_map/ppermute | solution.py:29
  11.5 11.5 %copy-start.6 = (bf16[4,256,256]{2,1,0:T(8,128)(2,1)S(1)}, bf16[4,256,256]{2,1,0:T(8,128)(2,1)}, u32[]{:S(2)}) copy-start(bf16[4,256,256]{2,1,0:T(8,128)(2,1)} %constant.2.clone.table_ref) | copy-start | bytes 1572868
  23.0 8.7 %collective-permute-start.4 = (f32[8,160,128]{2,1,0:T(8,128)S(1)}, f32[8,160,128]{2,1,0:T(8,128)S(1)}, u32[]{:S(2)}, u32[]{:S(2)}) collective-permute-start(f32[8,160,128]{2,1,0:T(8,128)S(1)} %get-tuple-element.23), channel_id=1, source_target_pairs={{0,15},{1,0},{2,1},{3,2},{4,3},{5,4},{6,5},{7,6},{8,7},{9,8},{10,9... | collective-permute-start | bytes 1966088 | tf_op jit(solution)/shard_map/ppermute | solution.py:29
  23.0 8.7 %copy-start.4 = (f32[4,128,128]{2,1,0:T(8,128)S(1)}, f32[4,128,128]{2,1,0:T(8,128)}, u32[]{:S(2)}) copy-start(f32[4,128,128]{2,1,0:T(8,128)} %pattern_ref.1) | copy-start | bytes 786436
  24.9 14.9 %collective-permute-start.5 = (f32[8,160,128]{2,1,0:T(8,128)S(1)}, f32[8,160,128]{2,1,0:T(8,128)S(1)}, u32[]{:S(2)}, u32[]{:S(2)}) collective-permute-start(f32[8,160,128]{2,1,0:T(8,128)S(1)} %get-tuple-element.29), channel_id=1, source_target_pairs={{0,15},{1,0},{2,1},{3,2},{4,3},{5,4},{6,5},{7,6},{8,7},{9,8},{10,9... | collective-permute-start | bytes 1966088 | tf_op jit(solution)/shard_map/ppermute | solution.py:29
  39.7 12.8 %collective-permute-start.6 = (f32[8,160,128]{2,1,0:T(8,128)S(1)}, f32[8,160,128]{2,1,0:T(8,128)S(1)}, u32[]{:S(2)}, u32[]{:S(2)}) collective-permute-start(f32[8,160,128]{2,1,0:T(8,128)S(1)} %get-tuple-element.30), channel_id=1, source_target_pairs={{0,1},{1,2},{2,3},{3,4},{4,5},{5,6},{6,7},{7,8},{8,9},{9,10},{10,1... | collective-permute-start | bytes 1966088 | tf_op jit(solution)/shard_map/ppermute | solution.py:29
where the time goes:
time: 56.1 us; the launch traced here: 55.6 us
  Pallas kernels  19.9 us (35%)
  waiting for transfers between devices  19.5 us (35%)
  starting transfers between devices  10 us (18%)
  local copies, waits for them, and re-layouts  5.29 us (9%)
  between operations  0.94 us (2%)
    ppermute x7, waiting for transfers between devices, shifted(): return lax.ppermute(x, axis, [(i, (i + by) % peers) for i in range(peers)])  19.5 us
    ppermute x7, starting transfers between devices, shifted(): return lax.ppermute(x, axis, [(i, (i + by) % peers) for i in range(peers)])  10 us
    pallas_call x2, Pallas kernels, gradients(): pl.pallas_call(functools.partial(wave_kernel, moved), out_shape=(jax.Shap...  9.87 us
    unnamed x15, local copies, waits for them, and re-layouts  4.16 us
    pallas_call x1, Pallas kernels, finish(): pl.pallas_call(finish_kernel, out_shape=jax.ShapeDtypeStruct(summed.shape...  2.95 us
    pallas_call x1, Pallas kernels, deposit(): pl.pallas_call(deposit_kernel, out_shape=jax.ShapeDtypeStruct(shape, F32)...  2.55 us
    pallas_call x1, Pallas kernels, pack_moved(): pl.pallas_call(pack_moved_kernel, out_shape=jax.ShapeDtypeStruct((planes,...  2.45 us
    pallas_call x1, Pallas kernels, parts(): pl.pallas_call(parts_kernel, out_shape=(jax.ShapeDtypeStruct((planes, CAP...  2.05 us
  transfers between devices with their start and end apart: 7, of which 3 were waited for; matrix products, arithmetic and copies ran while one was open for 5% of the time, Pallas kernels for 30%

commit v1 on v0

--- a/solution.py
+++ b/solution.py
@@ -12,7 +12,7 @@
 PS = 128
 PLANES = 8
 SLOTS = 4
-CAP = 160
+CAP_KEPT, CAP_MOVED = 152, 160
 F32 = jnp.float32
 
 N_KEPT, N_MOVED = 0, 1
@@ -21,6 +21,7 @@
 
 CHAINS = 4
 PACK_VMEM = 8 * 1024 * 1024
+PACK_MOVED_VMEM = 60 * 1024 * 1024
 WAVE_VMEM = 20 * 1024 * 1024
 
 
@@ -56,7 +57,7 @@
         most = jnp.maximum(up, down)
         score = (
             most
-            + jnp.where(most > CAP, 1 << 20, 0)
+            + jnp.where(jnp.logical_or(up > CAP_KEPT, down > CAP_MOVED), 1 << 20, 0)
             + jnp.where(kept > 2, 1 << 10, 0)
             + jnp.where(moved > 2, 1 << 10, 0)
         )
@@ -152,7 +153,7 @@
                 )
                 packed[plane, pl.ds(PS + offset - row, PS), :] = value
 
-    packed_ref[...] = packed[:, PS : PS + CAP, :]
+    packed_ref[...] = packed[:, PS : PS + CAP_MOVED, :]
 
 
 def pack_moved(positions, counts, tile):
@@ -160,16 +161,16 @@
     smem = pl.BlockSpec(memory_space=pltpu.SMEM)
     return pl.pallas_call(
         pack_moved_kernel,
-        out_shape=jax.ShapeDtypeStruct((planes, CAP, PS), F32),
+        out_shape=jax.ShapeDtypeStruct((planes, CAP_MOVED, PS), F32),
         in_specs=[smem, smem, pl.BlockSpec(memory_space=pl.ANY)],
         out_specs=pl.BlockSpec(memory_space=pltpu.VMEM),
         scratch_shapes=[
             pltpu.SMEM((PLAN,), jnp.int32),
             pltpu.VMEM((SLOTS, planes, rows, 2 * PS), F32),
-            pltpu.VMEM((planes, CAP + 2 * PS, PS), F32),
+            pltpu.VMEM((planes, CAP_MOVED + 2 * PS, PS), F32),
             pltpu.SemaphoreType.DMA((SLOTS,)),
         ],
-        compiler_params=pltpu.CompilerParams(vmem_limit_bytes=PACK_VMEM),
+        compiler_params=pltpu.CompilerParams(vmem_limit_bytes=PACK_MOVED_VMEM),
         cost_estimate=pl.CostEstimate(flops=0, bytes_accessed=4 * 1024 * 1024, transcendentals=0),
         name="pack_moved",
     )(positions, counts, tile)
@@ -187,7 +188,7 @@
         for plane in range(PLANES):
             packed[plane, pl.ds(offset, PS), :] = read_columns(tile_ref, plane, col)
 
-    packed_ref[...] = packed[:, :CAP, :]
+    packed_ref[...] = packed[:, :CAP_KEPT, :]
     write_plan(pos_ref, count_ref, plan)
 
     @pl.loop(0, plan[N_KEPT])
@@ -206,16 +207,15 @@
     smem = pl.BlockSpec(memory_space=pltpu.SMEM)
     vmem = pl.BlockSpec(memory_space=pltpu.VMEM)
     windows = jax.ShapeDtypeStruct((SLOTS, planes, PS, PS), F32)
+    numbers = jax.ShapeDtypeStruct((PLAN,), jnp.int32)
     return pl.pallas_call(
         parts_kernel,
-        out_shape=(jax.ShapeDtypeStruct((planes, CAP, PS), F32), windows, windows),
+        out_shape=(
+            jax.ShapeDtypeStruct((planes, CAP_KEPT, PS), F32), windows, windows, numbers, numbers
+        ),
         in_specs=[smem] * 4 + [vmem],
-        out_specs=(vmem, vmem, vmem),
-        scratch_shapes=[
-            pltpu.SMEM((PLAN,), jnp.int32),
-            pltpu.SMEM((PLAN,), jnp.int32),
-            pltpu.VMEM((planes, CAP + PS, PS), F32),
-        ],
+        out_specs=(vmem, vmem, vmem, smem, smem),
+        scratch_shapes=[pltpu.VMEM((planes, CAP_KEPT + PS, PS), F32)],
         compiler_params=pltpu.CompilerParams(vmem_limit_bytes=PACK_VMEM),
         cost_estimate=pl.CostEstimate(flops=0, bytes_accessed=8 * 1024 * 1024, transcendentals=0),
         name="parts",
@@ -255,12 +255,12 @@
 
 
 def wave_kernel(
-    moved, pos_ref, count_ref, own_ref, msg_ref, pattern_ref, probe_ref, prop_ref, table_ref,
+    moved, plan_ref, own_ref, msg_ref, pattern_ref, probe_ref, prop_ref, table_ref,
     *refs,
 ):
-    grads_ref, out_ref, plan_ref, msg, patch, grad, waves, packed = refs[-8:]
-    write_plan(pos_ref, count_ref, plan_ref)
-    msg[:, :CAP, :] = msg_ref[...]
+    grads_ref, out_ref, msg, patch, grad, waves, packed = refs[-7:]
+    cap = msg_ref.shape[1]
+    msg[:, :cap, :] = msg_ref[...]
     base = MOVED if moved else KEPT
     count = plan_ref[N_MOVED if moved else N_KEPT]
     layers = PLANES // 2
@@ -333,10 +333,10 @@
                     start = 0 if moved else PS - row
                     packed[plane, pl.ds(offset, PS), :] = grad[i, plane, pl.ds(start, PS), :]
 
-    out_ref[...] = packed[:, :CAP, :]
-
-
-def gradients(moved, positions, counts, own, msg, patterns, probe, prop, tables, after=()):
+    out_ref[...] = packed[:, :cap, :]
+
+
+def gradients(moved, plan, own, msg, patterns, probe, prop, tables, after=()):
     planes = own.shape[1]
     smem = pl.BlockSpec(memory_space=pltpu.SMEM)
     vmem = pl.BlockSpec(memory_space=pltpu.VMEM)
@@ -344,31 +344,28 @@
         functools.partial(wave_kernel, moved),
         out_shape=(
             jax.ShapeDtypeStruct((SLOTS, planes, PS, PS), F32),
-            jax.ShapeDtypeStruct((planes, CAP, PS), F32),
+            jax.ShapeDtypeStruct(msg.shape, F32),
         ),
-        in_specs=[smem] * 2 + [vmem] * 6 + [pl.BlockSpec(memory_space=pl.ANY)] * len(after),
+        in_specs=[smem] + [vmem] * 6 + [pl.BlockSpec(memory_space=pl.ANY)] * len(after),
         out_specs=(vmem, vmem),
         scratch_shapes=[
-            pltpu.SMEM((PLAN,), jnp.int32),
-            pltpu.VMEM((planes, CAP + PS, PS), F32),
+            pltpu.VMEM((planes, msg.shape[1] + PS, PS), F32),
             pltpu.VMEM((CHAINS, planes, 3 * PS, PS), F32),
             pltpu.VMEM((CHAINS, planes, 2 * PS, PS), F32),
             pltpu.VMEM((planes // 2, CHAINS, PS, 2 * PS), F32),
-            pltpu.VMEM((planes, CAP + PS, PS), F32),
+            pltpu.VMEM((planes, msg.shape[1] + PS, PS), F32),
         ],
         compiler_params=pltpu.CompilerParams(vmem_limit_bytes=WAVE_VMEM),
         cost_estimate=pl.CostEstimate(
             flops=6 * 1024**3, bytes_accessed=8 * 1024 * 1024, transcendentals=0
         ),
         name="waves_moved" if moved else "waves_kept",
-    )(positions, counts, own, msg, patterns, probe, prop, tables, *after)
+    )(plan, own, msg, patterns, probe, prop, tables, *after)
 
 
 def deposit_kernel(
-    pos_ref, count_ref, pos_above_ref, count_above_ref, kept_ref, moved_ref, below_ref, out_ref, plan, above, shift
+    plan, above, kept_ref, moved_ref, below_ref, out_ref, shift
 ):
-    write_plan(pos_ref, count_ref, plan)
-    write_plan(pos_above_ref, count_above_ref, above)
     out_ref[...] = jnp.zeros_like(out_ref)
 
     @pl.loop(0, plan[N_KEPT])
@@ -387,7 +384,7 @@
             shift[plane, pl.ds(row, PS), :] = moved_ref[k, plane]
             add_columns(out_ref, plane, col, jnp.where(inside, shift[plane, PS : 2 * PS, :], 0.0))
 
-    shift[:, PS : PS + CAP, :] = below_ref[...]
+    shift[:, PS : PS + CAP_MOVED, :] = below_ref[...]
 
     @pl.loop(0, plan[N_MOVED])
     def _(k):
@@ -398,26 +395,24 @@
             add_columns(out_ref, plane, col, jnp.where(inside, value, 0.0))
 
 
-def deposit(where, kept, moved, from_below, shape):
+def deposit(plans, kept, moved, from_below, shape):
     planes = shape[0]
     smem = pl.BlockSpec(memory_space=pltpu.SMEM)
     vmem = pl.BlockSpec(memory_space=pltpu.VMEM)
     return pl.pallas_call(
         deposit_kernel,
         out_shape=jax.ShapeDtypeStruct(shape, F32),
-        in_specs=[smem] * 4 + [vmem] * 3,
+        in_specs=[smem] * 2 + [vmem] * 3,
         out_specs=vmem,
-        scratch_shapes=[pltpu.SMEM((PLAN,), jnp.int32)] * 2
-        + [pltpu.VMEM((planes, CAP + 2 * PS, PS), F32)],
+        scratch_shapes=[pltpu.VMEM((planes, CAP_MOVED + 2 * PS, PS), F32)],
         compiler_params=pltpu.CompilerParams(vmem_limit_bytes=PACK_VMEM),
         cost_estimate=pl.CostEstimate(flops=0, bytes_accessed=4 * 1024 * 1024, transcendentals=0),
         name="deposit",
-    )(*where, kept, moved, from_below)
-
-
-def finish_kernel(pos_ref, count_ref, sum_ref, msg_ref, out_ref, plan, total, msg, sems):
-    write_plan(pos_ref, count_ref, plan)
-    msg[:, :CAP, :] = msg_ref[...]
+    )(*plans, kept, moved, from_below)
+
+
+def finish_kernel(plan, sum_ref, msg_ref, out_ref, total, msg, sems):
+    msg[:, :CAP_KEPT, :] = msg_ref[...]
     copies = []
     for plane in range(PLANES):
         total[plane] = sum_ref[plane]
@@ -435,25 +430,24 @@
         copy.wait()
 
 
-def finish(positions_above, counts_above, summed, from_above):
+def finish(above, summed, from_above):
     planes = summed.shape[0]
     smem = pl.BlockSpec(memory_space=pltpu.SMEM)
     vmem = pl.BlockSpec(memory_space=pltpu.VMEM)
     return pl.pallas_call(
         finish_kernel,
         out_shape=jax.ShapeDtypeStruct(summed.shape, F32),
-        in_specs=[smem, smem, vmem, vmem],
+        in_specs=[smem, vmem, vmem],
         out_specs=pl.BlockSpec(memory_space=pl.ANY),
         scratch_shapes=[
-            pltpu.SMEM((PLAN,), jnp.int32),
             pltpu.VMEM(summed.shape, F32),
-            pltpu.VMEM((planes, CAP + PS, PS), F32),
+            pltpu.VMEM((planes, CAP_KEPT + PS, PS), F32),
             pltpu.SemaphoreType.DMA((planes,)),
         ],
         compiler_params=pltpu.CompilerParams(vmem_limit_bytes=PACK_VMEM),
         cost_estimate=pl.CostEstimate(flops=0, bytes_accessed=4 * 1024 * 1024, transcendentals=0),
         name="finish",
-    )(positions_above, counts_above, summed, from_above)
+    )(above, summed, from_above)
 
 
 def per_device(tile_object, probe_wave, propagator_phase, diffraction, positions, counts):
@@ -473,21 +467,21 @@
     )
     rows_above = shifted(down, "ty", 1)
     where = (positions, counts, positions_above, counts_above)
-    up, own_kept, own_moved = parts(where, tile)
+    up, own_kept, own_moved, plan, above = parts(where, tile)
     up, rows_above = lax.optimization_barrier((up, rows_above))
     rows_below = shifted(up, "ty", -1)
     moved, back_up = gradients(
-        True, positions_above, counts_above, own_moved, rows_above, patterns_above,
+        True, above, own_moved, rows_above, patterns_above,
         probe_wave, prop, tables,
     )
     from_below = shifted(back_up, "ty", -1)
     kept, back_down = gradients(
-        False, positions, counts, own_kept, rows_below, diffraction,
+        False, plan, own_kept, rows_below, diffraction,
         probe_wave, prop, tables, after=(moved,),
     )
     from_above = shifted(back_down, "ty", 1)
-    summed = deposit(where, kept, moved, from_below, tile.shape)
-    out = finish(positions_above, counts_above, summed, from_above)
+    summed = deposit((plan, above), kept, moved, from_below, tile.shape)
+    out = finish(above, summed, from_above)
     return out.reshape(tile_object.shape)
 
 

time: 56.1 us -> 54.2 us (0.966)
  Pallas kernels: 19.9 us -> 27.1 us
  starting transfers between devices: 10 us -> 3.27 us
  local copies, waits for them, and re-layouts: 5.29 us -> 2.72 us
  waiting for transfers between devices: 19.5 us -> 20.1 us
    ppermute x7, starting transfers between devices: 10 us -> 3.27 us  [shifted(): return lax.ppermute(x, axis, [(i, (i + by) % peers) for i in range(peers)])]
    pallas_call x2, Pallas kernels: 9.87 us -> 16.1 us  [gradients(): pl.pallas_call(functools.partial(wave_kernel, moved), out_shape=(jax.Shap...]
    unnamed x15 -> x11, local copies, waits for them, and re-layouts: 4.16 us -> 1.58 us
    pallas_call x1, Pallas kernels: 2.05 us -> 3.48 us  [parts(): pl.pallas_call(parts_kernel, out_shape=(jax.ShapeDtypeStruct((planes, CAP...]
    pallas_call x1, Pallas kernels: 2.45 us -> 3.3 us  [pack_moved(): pl.pallas_call(pack_moved_kernel, out_shape=jax.ShapeDtypeStruct((planes,...]
    pallas_call x1, Pallas kernels: 2.55 us -> 1.78 us  [deposit(): pl.pallas_call(deposit_kernel, out_shape=jax.ShapeDtypeStruct(shape, F32)...]
    ppermute x7, waiting for transfers between devices: 19.5 us -> 20.1 us  [shifted(): return lax.ppermute(x, axis, [(i, (i + by) % peers) for i in range(peers)])]
  transfers between devices with their start and end apart: 7 -> 7, of which waited for: 3 -> 4; matrix products, arithmetic and copies ran while one was open for 5% -> 5% of each run, Pallas kernels for 30% -> 46%
where the time goes in v1:
time: 54.2 us
  Pallas kernels  27.1 us (50%)
  waiting for transfers between devices  20.1 us (37%)
  starting transfers between devices  3.27 us (6%)
  local copies, waits for them, and re-layouts  2.72 us (5%)
  between operations  0.95 us (2%)
    ppermute x7, waiting for transfers between devices, shifted(): return lax.ppermute(x, axis, [(i, (i + by) % peers) for i in range(peers)])  20.1 us
    pallas_call x2, Pallas kernels, gradients(): pl.pallas_call(functools.partial(wave_kernel, moved), out_shape=(jax.Shap...  16.1 us
    pallas_call x1, Pallas kernels, parts(): pl.pallas_call(parts_kernel, out_shape=(jax.ShapeDtypeStruct((planes, CAP...  3.48 us
    pallas_call x1, Pallas kernels, pack_moved(): pl.pallas_call(pack_moved_kernel, out_shape=jax.ShapeDtypeStruct((planes,...  3.3 us
    ppermute x7, starting transfers between devices, shifted(): return lax.ppermute(x, axis, [(i, (i + by) % peers) for i in range(peers)])  3.27 us
    pallas_call x1, Pallas kernels, finish(): pl.pallas_call(finish_kernel, out_shape=jax.ShapeDtypeStruct(summed.shape...  2.42 us
    pallas_call x1, Pallas kernels, deposit(): pl.pallas_call(deposit_kernel, out_shape=jax.ShapeDtypeStruct(shape, F32)...  1.78 us
    unnamed x11, local copies, waits for them, and re-layouts  1.58 us
  transfers between devices with their start and end apart: 7, of which 4 were waited for; matrix products, arithmetic and copies ran while one was open for 5% of the time, Pallas kernels for 46%

profile of v1, /device:TPU:0, one launch (start us, length us, event | category | flops | bytes accessed | tf_op | source)
XLA Modules:
  0.0 54.2 jit_solution(3042486887538228556)
XLA Ops:
  0.0 0.0 copy-start.1
  0.0 0.0 copy-start
  0.0 0.5 collective-permute-start.2
  0.5 2.6 %collective-permute-start.1 = (s32[1]{0:T(128)}, s32[1]{0:T(128)}, u32[]{:S(2)}, u32[]{:S(2)}) collective-permute-start(s32[1]{0:T(128)} %param.12), channel_id=1, source_target_pairs={{0,1},{1,2},{2,3},{3,4},{4,5},{5,6},{6,7},{7,8},{8,9},{9,10},{10,1... | collective-permute-start | bytes 20 | tf_op jit(solution)/shard_map/ppermute | solution.py:30
  3.1 0.1 collective-permute-start
  3.8 3.3 %pack_moved.1 = f32[8,160,128]{2,1,0:T(8,128)} custom-call(s32[2,4]{1,0:T(2,128)} %bitcast.14, s32[1]{0:T(128)S(6)} %copy.10.count_ref, f32[8,128,768]{2,1,0:T(8,128)} %bitcast.11), custom_call_target="tpu_custom_call" | custom-call | bytes 4194304 | tf_op jit(solution)/shard_map/pack_moved/pallas_call | solution.py:162
  7.1 0.0 copy-start.3
  7.1 2.6 %collective-permute-done.1.count_above_ref = s32[1]{0:T(128)} collective-permute-done((s32[1]{0:T(128)}, s32[1]{0:T(128)}, u32[]{:S(2)}, u32[]{:S(2)}) %collective-permute-start.1) | collective-permute-done | bytes 36 | tf_op jit(solution)/shard_map/ppermute | solution.py:30
  9.7 0.0 collective-permute-done.pos_above_ref
  9.8 0.0 collective-permute-done.2.pattern_ref
  9.8 0.0 collective-permute-start.3
  9.8 1.6 %copy.8 = f32[128,128]{0,1:T(8,128)} copy(f32[128,128]{1,0:T(8,128)} %param.9) | data formatting | bytes 131072 | tf_op args[2]
  11.3 0.0 copy-start.4
  11.3 1.1 %cosine_bitcast_fusion = (f32[1,128,128]{2,1,0:T(8,128)S(1)}, f32[1,128,128]{2,1,0:T(8,128)S(1)}) fusion(f32[128,128]{0,1:T(8,128)} %copy.8), kind=kLoop, calls=%fused_computation.2 | loop fusion | bytes 196608 | tf_op jit(solution)/shard_map/stack | solution.py:461
  12.5 0.0 copy-done.1
  12.5 0.0 copy-done
  12.5 3.5 %parts.1 = (f32[8,152,128]{2,1,0:T(8,128)S(1)}, f32[4,8,128,128]{3,2,1,0:T(8,128)S(1)}, f32[4,8,128,128]{3,2,1,0:T(8,128)S(1)}, s32[128]{0:T(128)S(1)}, s32[128]{0:T(128)S(1)}) custom-call(s32[2,4]{1,0:T(2,128)S(1)} %bitcast.15, s32[1]{0:T(128)S(6)} %copy.10.count_ref, s32[2,4]{1,0:T(2,128)S(1)} %collective-permute-done.pos_above_ref, ...), custom_call_target="tpu_custom_call" | custom-call | bytes 8388608 | tf_op jit(solution)/shard_map/parts/pallas_call | solution.py:211
  16.0 6.9 %collective-permute-done.3.msg_ref = f32[8,160,128]{2,1,0:T(8,128)} collective-permute-done((f32[8,160,128]{2,1,0:T(8,128)}, f32[8,160,128]{2,1,0:T(8,128)}, u32[]{:S(2)}, u32[]{:S(2)}) %collective-permute-start.3) | collective-permute-done | bytes 655392 | tf_op jit(solution)/shard_map/ppermute | solution.py:30
  22.9 0.0 collective-permute-start.4
  22.9 0.0 copy-done.3
  22.9 0.0 copy-done.4
  22.9 0.0 copy-start.2
  22.9 8.2 %waves_moved.1 = (f32[4,8,128,128]{3,2,1,0:T(8,128)S(1)}, f32[8,160,128]{2,1,0:T(8,128)S(1)}) custom-call(s32[128]{0:T(128)S(1)} %get-tuple-element.22.plan_ref.above.plan, f32[4,8,128,128]{3,2,1,0:T(8,128)S(1)} %get-tuple-element.28.own_ref, f32[8,160,128]{2,1,0:T(8,128)} %collective-permute-done.3.msg_ref, ...), custom_call_target="tpu_custom_call" | custom-call | flops 6442450944 | bytes 8388608 | tf_op jit(solution)/shard_map/waves_moved/pallas_call | solution.py:343
  31.2 0.1 collective-permute-start.5
  31.2 0.0 collective-permute-done.4.msg_ref
  31.2 0.0 copy-done.2
  31.3 7.9 %waves_kept.1 = (f32[4,8,128,128]{3,2,1,0:T(8,128)S(1)}, f32[8,152,128]{2,1,0:T(8,128)S(1)}) custom-call(s32[128]{0:T(128)S(1)} %get-tuple-element.23.plan_ref.plan, f32[4,8,128,128]{3,2,1,0:T(8,128)S(1)} %get-tuple-element.24.own_ref, f32[8,152,128]{2,1,0:T(8,128)S(1)} %collective-permute-done.4.msg_ref, f32[4,128,128]{2,1,0:T(8,128)S(1)} %copy-done.2, ...), custom_call_target="tpu_custom_call" | custom-call | flops 6442450944 | bytes 8388608 | tf_op jit(solution)/shard_map/waves_kept/pallas_call | solution.py:343
  39.2 0.1 collective-permute-start.6
  39.3 0.1 collective-permute-done.5.below_ref
  39.3 1.8 %deposit.1.sum_ref = f32[8,128,768]{2,1,0:T(8,128)S(1)} custom-call(s32[128]{0:T(128)S(1)} %get-tuple-element.23.plan_ref.plan, s32[128]{0:T(128)S(1)} %get-tuple-element.22.plan_ref.above.plan, f32[4,8,128,128]{3,2,1,0:T(8,128)S(1)} %get-tuple-element.32.kept_ref, f32[4,8,128,128]{3,2,1,0:T(8,128)S(1)} %get-tuple-element.31.refs_0_.moved_ref, ...), custom_call_target="tpu_custom_call" | custom-call | bytes 4194304 | tf_op jit(solution)/shard_map/deposit/pallas_call | solution.py:402
  41.1 10.5 %collective-permute-done.6.msg_ref = f32[8,152,128]{2,1,0:T(8,128)S(1)} collective-permute-done((f32[8,152,128]{2,1,0:T(8,128)S(1)}, f32[8,152,128]{2,1,0:T(8,128)S(1)}, u32[]{:S(2)}, u32[]{:S(2)}) %collective-permute-start.6) | collective-permute-done | bytes 622624 | tf_op jit(solution)/shard_map/ppermute | solution.py:30
  51.6 2.4 %finish.1 = f32[8,128,768]{2,1,0:T(8,128)} custom-call(s32[128]{0:T(128)S(1)} %get-tuple-element.22.plan_ref.above.plan, f32[8,128,768]{2,1,0:T(8,128)S(1)} %deposit.1.sum_ref, f32[8,152,128]{2,1,0:T(8,128)S(1)} %collective-permute-done.6.msg_ref), custom_call_target="tpu_custom_call" | custom-call | bytes 4194304 | tf_op jit(solution)/shard_map/finish/pallas_call | solution.py:437
  (1 shorter events, 0.0 us)
Async XLA Ops:
  0.0 12.5 %copy-start.1 = (s32[4,2]{0,1:T(2,128)S(1)}, s32[4,2]{0,1:T(2,128)}, u32[]{:S(2)}) copy-start(s32[4,2]{0,1:T(2,128)} %param.11) | copy-start | bytes 100
  0.0 12.5 %copy-start = (f32[4,2,128,768]{3,2,1,0:T(8,128)S(1)}, f32[4,2,128,768]{3,2,1,0:T(8,128)}, u32[]{:S(2)}) copy-start(f32[4,2,128,768]{3,2,1,0:T(8,128)} %param.7) | copy-start | bytes 9437188
  0.0 9.8 %collective-permute-start.2 = (f32[4,128,128]{2,1,0:T(8,128)}, f32[4,128,128]{2,1,0:T(8,128)S(1)}, u32[]{:S(2)}, u32[]{:S(2)}) collective-permute-start(f32[4,128,128]{2,1,0:T(8,128)} %pattern_ref.1), channel_id=1, source_target_pairs={{0,1},{1,2},{2,3},{3,4},{4,5},{5,6},{6,7},{7,8},{8,9},{9,10},{10,1... | collective-permute-start | bytes 786440 | tf_op jit(solution)/shard_map/ppermute | solution.py:30
  0.5 9.3 %collective-permute-start.1 = (s32[1]{0:T(128)}, s32[1]{0:T(128)}, u32[]{:S(2)}, u32[]{:S(2)}) collective-permute-start(s32[1]{0:T(128)} %param.12), channel_id=1, source_target_pairs={{0,1},{1,2},{2,3},{3,4},{4,5},{5,6},{6,7},{7,8},{8,9},{9,10},{10,1... | collective-permute-start | bytes 20 | tf_op jit(solution)/shard_map/ppermute | solution.py:30
  3.1 6.7 %collective-permute-start = (s32[2,4]{1,0:T(2,128)}, s32[2,4]{1,0:T(2,128)S(1)}, u32[]{:S(2)}, u32[]{:S(2)}) collective-permute-start(s32[2,4]{1,0:T(2,128)} %bitcast.13), channel_id=1, source_target_pairs={{0,1},{1,2},{2,3},{3,4},{4,5},{5,6},{6,7},{7,8},{8,9},{9,10},{10,1... | collective-permute-start | bytes 104 | tf_op jit(solution)/shard_map/ppermute | solution.py:30
  7.1 15.8 %copy-start.3 = (f32[2,128,128]{2,1,0:T(8,128)S(1)}, f32[2,128,128]{2,1,0:T(8,128)}, u32[]{:S(2)}) copy-start(f32[2,128,128]{2,1,0:T(8,128)} %probe_ref.3) | copy-start | bytes 393220
  9.8 13.1 %collective-permute-start.3 = (f32[8,160,128]{2,1,0:T(8,128)}, f32[8,160,128]{2,1,0:T(8,128)}, u32[]{:S(2)}, u32[]{:S(2)}) collective-permute-start(f32[8,160,128]{2,1,0:T(8,128)} %pack_moved.1), channel_id=1, source_target_pairs={{0,1},{1,2},{2,3},{3,4},{4,5},{5,6},{6,7},{7,8},{8,9},{9,10},{10,1... | collective-permute-start | bytes 1966088 | tf_op jit(solution)/shard_map/ppermute | solution.py:30
  11.3 11.6 %copy-start.4 = (bf16[4,256,256]{2,1,0:T(8,128)(2,1)S(1)}, bf16[4,256,256]{2,1,0:T(8,128)(2,1)}, u32[]{:S(2)}) copy-start(bf16[4,256,256]{2,1,0:T(8,128)(2,1)} %constant.2.clone.table_ref) | copy-start | bytes 1572868
  22.9 8.3 %collective-permute-start.4 = (f32[8,152,128]{2,1,0:T(8,128)S(1)}, f32[8,152,128]{2,1,0:T(8,128)S(1)}, u32[]{:S(2)}, u32[]{:S(2)}) collective-permute-start(f32[8,152,128]{2,1,0:T(8,128)S(1)} %get-tuple-element.27), channel_id=1, source_target_pairs={{0,15},{1,0},{2,1},{3,2},{4,3},{5,4},{6,5},{7,6},{8,7},{9,8},{10,9... | collective-permute-start | bytes 1867784 | tf_op jit(solution)/shard_map/ppermute | solution.py:30
  22.9 8.3 %copy-start.2 = (f32[4,128,128]{2,1,0:T(8,128)S(1)}, f32[4,128,128]{2,1,0:T(8,128)}, u32[]{:S(2)}) copy-start(f32[4,128,128]{2,1,0:T(8,128)} %pattern_ref.1) | copy-start | bytes 786436
  31.2 8.2 %collective-permute-start.5 = (f32[8,160,128]{2,1,0:T(8,128)S(1)}, f32[8,160,128]{2,1,0:T(8,128)S(1)}, u32[]{:S(2)}, u32[]{:S(2)}) collective-permute-start(f32[8,160,128]{2,1,0:T(8,128)S(1)} %get-tuple-element.33), channel_id=1, source_target_pairs={{0,15},{1,0},{2,1},{3,2},{4,3},{5,4},{6,5},{7,6},{8,7},{9,8},{10,9... | collective-permute-start | bytes 1966088 | tf_op jit(solution)/shard_map/ppermute | solution.py:30
  39.2 12.4 %collective-permute-start.6 = (f32[8,152,128]{2,1,0:T(8,128)S(1)}, f32[8,152,128]{2,1,0:T(8,128)S(1)}, u32[]{:S(2)}, u32[]{:S(2)}) collective-permute-start(f32[8,152,128]{2,1,0:T(8,128)S(1)} %get-tuple-element.34), channel_id=1, source_target_pairs={{0,1},{1,2},{2,3},{3,4},{4,5},{5,6},{6,7},{7,8},{8,9},{9,10},{10,1... | collective-permute-start | bytes 1867784 | tf_op jit(solution)/shard_map/ppermute | solution.py:30
